TPU v7x, 256 devices: a whole 4x4x8 slice. The times are simulated.
256 devices in a mesh: dp: 16 (over y_lo, z), ctx: 16 (over y_hi, x, core).
Axes of the slice: x: 4, y: 4 (y_hi: 2, y_lo: 2; y = y_hi * 2 + y_lo), z: 8, core: 2. Of those that a mesh axis runs over, the one named last changes fastest.
Arguments:
- inputs: bfloat16 [16, 2048, 4096], P('dp', 'ctx'), may hold values from -6 to 6
- out_grads: bfloat16 [16, 2048, 1024], P('dp', 'ctx'), may hold values from -8 to 8
- basis_in: bfloat16 [4096, 4096], P(None, 'ctx'), may hold values from -0.09375 to 0.09375
- basis_out: bfloat16 [1024, 1024], replicated, may hold values from -0.1875 to 0.1875
Outputs:
- corrected: float32 [1024, 4096], P('dp', 'ctx')
All inputs are finite; a program needn't handle non-finite values.
Results may differ from a plain program's by a relative error of at most 0.002.
Values may be sent and summed in bfloat16 or wider, within the bound.
A program may use at most 128 MiB of HBM per device.

v0:
```python
import jax
import jax.numpy as jnp
from jax import lax
from jax.sharding import PartitionSpec as P


def tile_update(acts, grads, basis_in):
    rot_in = jnp.dot(acts, basis_in, preferred_element_type=jnp.float32).astype(jnp.bfloat16)
    return lax.dot_general(
        grads, rot_in, (((0,), (0,)), ((), ())), preferred_element_type=jnp.float32
    )


def local(inputs, out_grads, basis_in, basis_out):
    outputs = out_grads.shape[2]
    rot_out = jnp.dot(
        lax.all_gather(out_grads[0], "ctx", axis=0, tiled=True),
        basis_out,
        preferred_element_type=jnp.float32,
    ).astype(jnp.bfloat16)
    tile = tile_update(lax.all_gather(inputs[0], "ctx", axis=0, tiled=True), rot_out, basis_in)
    squares = tile * tile
    scale = 1.0 / (inputs.shape[1] * lax.axis_size("ctx") * inputs.shape[0] * lax.axis_size("dp"))
    whole = lax.psum(squares, "dp")
    rows = outputs // lax.axis_size("dp")
    summed = lax.dynamic_slice_in_dim(whole, lax.axis_index("dp") * rows, rows, 0)
    return summed * scale


def solution(mesh):
    return jax.shard_map(
        local,
        mesh=mesh,
        in_specs=(P("dp", "ctx", None), P("dp", "ctx", None), P(None, "ctx"), P()),
        out_specs=P("dp", "ctx"),
        check_vma=False,
    )
```

profile of v0, /device:TPU:2, one launch (start us, length us, event | category | flops | bytes accessed | tf_op | source)
XLA Modules:
  0.0 345.9 jit_solution(5069264686948266568)
XLA Ops:
  6.5 0.0 copy-start
  6.5 0.0 all-gather.7.cloned.1.call-start
  6.5 0.7 all-gather.7.cloned.1.call-update
  7.3 0.0 all-gather.5.cloned.1.call-start
  7.3 0.7 all-gather.5.cloned.1.call-update
  8.0 0.0 all-reduce.2.cloned.1.call-start
  8.1 119.1 %all-gather.7.cloned.1.call-done = bf16[1,2048,4096]{2,1,0:T(8,128)(2,1)} async-done(((bf16[1,128,4096]{2,1,0:T(8,128)(2,1)}), bf16[1,2048,4096]{2,1,0:T(8,128)(2,1)}) %all-gather.7.cloned.1.call-update) | async-done | bytes 16777232 | tf_op jit(solution)/shard_map/all_gather | solution.py:21
  127.1 0.0 copy-done
  127.1 8.2 %fusion.6 = bf16[2048,256]{1,0:T(8,128)(2,1)S(1)} fusion(bf16[4096,256]{1,0:T(8,128)(2,1)S(1)} %copy-done, bf16[1,2048,4096]{2,1,0:T(8,128)(2,1)} %all-gather.7.cloned.1.call-done), kind=kOutput, calls=%fused_computation.6 | convolution fusion | flops 4295491584 | bytes 19922944 | tf_op jit(solution)/shard_map/dot_general | solution.py:8
  135.4 54.5 %all-gather.5.cloned.1.call-done = bf16[1,2048,1024]{2,1,0:T(8,128)(2,1)} async-done(((bf16[1,128,1024]{2,1,0:T(8,128)(2,1)}), bf16[1,2048,1024]{2,1,0:T(8,128)(2,1)}) %all-gather.5.cloned.1.call-update) | async-done | bytes 4194320 | tf_op jit(solution)/shard_map/all_gather | solution.py:17
  189.9 11.1 %fusion.13 = f32[1024,256]{1,0:T(8,128)} fusion(bf16[2048,256]{1,0:T(8,128)(2,1)S(1)} %fusion.6, bf16[1024,1024]{1,0:T(8,128)(2,1)} %param.7, bf16[1,2048,1024]{2,1,0:T(8,128)(2,1)} %all-gather.5.cloned.1.call-done), kind=kOutput, calls=%fused_computation.7 | convolution fusion | flops 5371068416 | bytes 8388608 | tf_op jit(solution)/shard_map/dot_general | solution.py:9
  201.0 0.0 all-reduce.2.cloned.1.call-update
  201.0 136.9 %all-reduce.2.cloned.1.call-done = f32[1024,256]{1,0:T(8,128)} async-done(((f32[1024,256]{1,0:T(8,128)}), f32[1024,256]{1,0:T(8,128)}) %all-reduce.2.cloned.1.call-update) | async-done | bytes 1048592 | tf_op jit(solution)/shard_map/psum | solution.py:24
  337.9 1.5 dynamic-slice_multiply_fusion
Async XLA Ops:
  6.5 120.6 %copy-start = (bf16[4096,256]{1,0:T(8,128)(2,1)S(1)}, bf16[4096,256]{1,0:T(8,128)(2,1)}, u32[]{:S(2)}) copy-start(bf16[4096,256]{1,0:T(8,128)(2,1)} %param.6) | copy-start | bytes 6291460
  6.5 120.6 %all-gather.7.cloned.1.call-start = ((), (), s32[]{:S(2)}) async-start(), calls=%async_computation.2 | async-start | bytes 17825792 | tf_op jit(solution)/shard_map/all_gather | solution.py:21
  7.3 182.6 %all-gather.5.cloned.1.call-start = ((), (), s32[]{:S(2)}) async-start(), calls=%async_computation.1 | async-start | bytes 4456448 | tf_op jit(solution)/shard_map/all_gather | solution.py:17
  8.0 329.9 %all-reduce.2.cloned.1.call-start = ((), (), s32[]{:S(2)}) async-start(), calls=%async_computation | async-start | bytes 2097152 | tf_op jit(solution)/shard_map/psum | solution.py:24
Sparse Core Ops, SparseCore 0:
  10.1 116.9 all-gather.6
  129.8 59.9 all-gather.4
  201.1 136.7 all-reduce.1
where the time goes:
time: 346 us
  waiting for transfers between devices  312 us (90%)
  matrix products  19.3 us (6%)
  between operations  13.1 us (4%)
    psum x1, waiting for transfers between devices, local(): whole = lax.psum(squares, 'dp')  137 us
    all_gather x1, waiting for transfers between devices, local(): lax.all_gather(inputs[0], 'ctx', axis=0, tiled=True)  119 us
    all_gather x1, waiting for transfers between devices, local(): lax.all_gather(out_grads[0], 'ctx', axis=0, tiled=True)  54.5 us
    dot_general x1, matrix products, tile_update(): lax.dot_general(grads, rot_in, (((0,), (0,)), ((), ())), preferred_elemen...  11.1 us
    dot_general x1, matrix products, tile_update(): jnp.dot(acts, basis_in, preferred_element_type=jnp.float32)  8.23 us
  transfers between devices with their start and end apart: 3, of which 3 were waited for; matrix products, arithmetic and copies ran while one was open for 2% of the time, Pallas kernels for 0%

commit v1 on v0

v1 whole, which is shorter than its diff:
```python
import functools

import jax
import jax.numpy as jnp
from jax import lax
from jax.experimental import pallas as pl
from jax.experimental.pallas import tpu as pltpu
from jax.sharding import PartitionSpec as P

MESH = pl.DeviceIdType.MESH
BF16, F32 = jnp.bfloat16, jnp.float32
CHUNKS = ((0, 1), (1, 1), (2, 2), (4, 2), (6, 2))
GROUPS = ((0, 4), (4, 4))
N_SEND = 256
N_RECV = 256


class Sems:
    def __init__(self, send, recv):
        self.send, self.recv, self.n_send, self.slots = send, recv, 0, {}

    def out(self):
        self.n_send += 1
        return self.send.at[self.n_send - 1]

    def into(self, *name):
        return self.recv.at[self.slots.setdefault(name, len(self.slots))]


def kernel(
    scale, x_hbm, g_hbm, bi_hbm, bo_hbm, o_ref,
    xbuf, gbuf, bobuf, rbuf, rsend, psend, precv, pkeep, hz, hbuf, bbuf, acc, ssend, rr,
    send_sem, recv_sem, fin_sem,
):
    dp, ctx = lax.axis_index("dp"), lax.axis_index("ctx")
    yl, z = dp // 8, dp % 8
    a, b, c = ctx // 8, (ctx // 2) % 4, ctx % 2
    right, left = (b + 1) % 4, (b + 3) % 4
    sems = Sems(send_sem, recv_sem)
    pending = []

    def dev(a=a, yl=yl, z=z, b=b, c=c):
        return (yl * 8 + z, a * 8 + b * 2 + c)

    sibling = dev(c=1 - c)

    def send(src, dst, to, *name):
        copy = pltpu.make_async_remote_copy(
            src_ref=src, dst_ref=dst, send_sem=sems.out(), recv_sem=sems.into(*name),
            device_id=to, device_id_type=MESH,
        )
        copy.start()
        pending.append(copy)

    def wait(ref, *name):
        pltpu.make_async_copy(ref, ref, sems.into(*name)).wait()

    def local(src, dst, *name):
        copy = pltpu.make_async_copy(src, dst, sems.into(*name))
        copy.start()
        return copy

    def flush():
        while pending:
            pending.pop(0).wait_send()

    peers = [dev(b=(b + i) % 4, c=k) for i in (1, 3) for k in (0, 1)]
    peers += [dev(b=(b + 2) % 4), sibling]
    peers += [dev(z=(z + i) % 8) for i in range(1, 8)]
    peers += [
        dev(a=(a + i) % 2, yl=(yl + j) % 2, c=k)
        for i, j in ((0, 1), (1, 0), (1, 1))
        for k in (0, 1)
    ]
    barrier = pltpu.get_barrier_semaphore()
    for peer in peers:
        pl.semaphore_signal(barrier, inc=1, device_id=peer, device_id_type=MESH)
    own, partner = a * 2 + c, (1 - a) * 2 + c
    load_g = local(g_hbm.at[0], gbuf, "g")
    load_bo = local(bo_hbm, bobuf, "bo")
    features = pl.ds(pl.multiple_of(b * 1024, 1024), 1024)
    load_x = local(x_hbm.at[0, :, features], xbuf.at[c, b], "x")
    load_bi = local(bi_hbm, bbuf.at[own], "bi")
    pl.semaphore_wait(barrier, len(peers))

    def x_send(j):
        lo, n = CHUNKS[j]
        for i in (1, 3, 2):
            to = (b + i) % 4
            src = pl.ds(pl.multiple_of(to * 1024 + lo * 128, 128), n * 128)
            send(
                x_hbm.at[0, :, src], xbuf.at[c, b, :, pl.ds(lo * 128, n * 128)],
                dev(b=to), "X", j, i,
            )

    def b_send(g):
        lo, n = GROUPS[g]
        at = (pl.ds(2 * (1 - yl), 2), pl.ds(lo * 128, n * 128))
        send(bi_hbm.at[at], bbuf.at[(own, *at)], dev(a=1 - a, yl=1 - yl), "B1", g)

    def b_forward(g):
        lo, n = GROUPS[g]
        at = (partner, pl.ds(2 * yl, 2), pl.ds(lo * 128, n * 128))
        wait(bbuf.at[at], "B1", g)
        send(bbuf.at[at], bbuf.at[at], dev(yl=1 - yl), "B2", g)

    def b_share(g):
        lo, n = GROUPS[g]
        at = (partner, pl.ds(2 * (1 - yl), 2), pl.ds(lo * 128, n * 128))
        wait(bbuf.at[at], "B2", g)
        at = (partner, slice(None), pl.ds(lo * 128, n * 128))
        send(bbuf.at[at], bbuf.at[at], sibling, "B3", g)

    def b_done(g):
        lo, n = GROUPS[g]
        wait(bbuf.at[(3 - own) % 4, :, pl.ds(lo * 128, n * 128)], "B3", g)

    x_send(0)
    b_send(0)

    load_g.wait()
    load_bo.wait()
    for k in range(2):
        rot = jnp.dot(gbuf[...], bobuf[:, 512 * k : 512 * k + 512], preferred_element_type=F32)
        turned = rot.T.astype(BF16).reshape(8, 2, 32, 128)
        for h in range(2):
            rsend[k, h] = turned[:, h].reshape(256, 128)
    slot = c * 4 + b
    for i in (1, 3):
        to = (b + i) % 4
        send(rsend.at[c], rbuf.at[slot], dev(b=to), "R", i, 0)
        send(rsend.at[1 - c], rbuf.at[slot], dev(b=to, c=1 - c), "R", i, 1)
    send(rsend.at[1 - c], rbuf.at[slot], sibling, "R", 0, 1)
    rbuf[slot] = rsend[c]
    send(bi_hbm, bbuf.at[own], sibling, "B0")
    x_send(1)

    def r_forward(i, origin, to):
        same, other = c * 4 + origin, (1 - c) * 4 + origin
        wait(rbuf.at[same], "R", i, 0)
        wait(rbuf.at[other], "R", i, 1)
        first = 0 if i == 1 else 4
        send(rbuf.at[first + origin], rbuf.at[first + origin], dev(b=to), "R", 2, i)

    r_forward(1, left, right)
    r_forward(3, right, left)
    x_send(2)
    b_forward(0)
    x_send(3)
    x_send(4)
    far = (b + 2) % 4
    wait(rbuf.at[far], "R", 2, 1)
    wait(rbuf.at[4 + far], "R", 2, 3)
    wait(rbuf.at[(1 - c) * 4 + b], "R", 0, 1)
    load_x.wait()

    def A(j):
        lo, n = CHUNKS[j]
        columns = pl.ds(lo * 128, n * 128)
        for i in (1, 3, 2):
            wait(xbuf.at[c, (b + 4 - i) % 4, :, columns], "X", j, i)
        at = (c, slice(None), slice(None), columns)
        send(xbuf.at[at], xbuf.at[at], sibling, "XF", j)

    def B(j):
        lo, n = CHUNKS[j]
        columns = pl.ds(lo * 128, n * 128)
        wait(xbuf.at[1 - c, :, :, columns], "XF", j)

        def product(half):
            lhs = jnp.concatenate([rbuf[s, half] for s in range(8)], axis=1)
            rhs = xbuf[:, :, :, lo * 128 : (lo + n) * 128].reshape(1024, n * 128)
            return jnp.dot(lhs, rhs, preferred_element_type=F32)

        theirs = product(1 - a).astype(BF16)
        for i in range(n):
            psend[lo + i] = theirs[:, i * 128 : (i + 1) * 128]
        at = pl.ds(lo, n)
        send(psend.at[at], precv.at[at], dev(a=1 - a), "P", j)
        mine = product(a)
        for i in range(n):
            pkeep[lo + i] = mine[:, i * 128 : (i + 1) * 128]

    def C(j):
        lo, n = CHUNKS[j]
        at = pl.ds(lo, n)
        wait(precv.at[at], "P", j)
        hz[lo : lo + n] = (pkeep[lo : lo + n] + precv[lo : lo + n].astype(F32)).astype(BF16)
        rows = pl.ds(pl.multiple_of(z * 32, 32), 32)
        for i in (4, 3, 5, 2, 6, 1, 7):
            to = (z + i) % 8
            theirs = pl.ds(pl.multiple_of(to * 32, 32), 32)
            send(hz.at[at, theirs], hbuf.at[b, at, rows], dev(z=to), "Z", j, i)
        for i in range(n):
            hbuf[b, lo + i, rows] = hz[lo + i, rows]

    def D(j):
        lo, n = CHUNKS[j]
        at = pl.ds(lo, n)
        for i in range(1, 8):
            rows = pl.ds(pl.multiple_of((z + 8 - i) % 8 * 32, 32), 32)
            wait(hbuf.at[b, at, rows], "Z", j, i)
        send(hbuf.at[b, at], hbuf.at[b, at], dev(b=right), "H", j, 1)
        send(hbuf.at[b, at], hbuf.at[b, at], dev(b=left), "H", j, 3)

    def E(j):
        lo, n = CHUNKS[j]
        at = pl.ds(lo, n)
        wait(hbuf.at[left, at], "H", j, 1)
        half = hbuf.at[left, at, pl.ds(0, 128)]
        send(half, half, dev(b=right), "HF", j, 1)
        wait(hbuf.at[right, at], "H", j, 3)
        half = hbuf.at[right, at, pl.ds(128, 128)]
        send(half, half, dev(b=left), "HF", j, 3)

    def F(j):
        lo, n = CHUNKS[j]
        at = pl.ds(lo, n)
        wait(hbuf.at[far, at, pl.ds(0, 128)], "HF", j, 1)
        wait(hbuf.at[far, at, pl.ds(128, 128)], "HF", j, 3)
        lhs = jnp.concatenate(
            [hbuf[x, lo + i] for x in range(4) for i in range(n)], axis=1
        )
        for k in range(4):
            rhs = bbuf[k, :, lo * 128 : (lo + n) * 128].reshape(n * 512, 256)
            term = jnp.dot(lhs, rhs, preferred_element_type=F32)
            acc[k] = term if j == 0 else acc[k] + term

    A(0)
    B(0)
    A(1)
    B(1)
    C(0)
    A(2)
    B(2)
    C(1)
    D(0)
    A(3)
    B(3)
    C(2)
    D(1)
    A(4)
    B(4)
    b_send(1)
    b_share(0)
    E(0)
    C(3)
    D(2)
    E(1)
    C(4)
    load_bi.wait()
    wait(bbuf.at[a * 2 + 1 - c], "B0")
    b_done(0)
    F(0)
    D(3)
    F(1)
    E(2)
    b_forward(1)
    D(4)
    b_share(1)
    F(2)
    E(3)
    b_done(1)
    F(3)
    E(4)
    flush()
    F(4)

    for k in range(4):
        tile = acc[k]
        ssend[k] = (tile * tile).reshape(8, 32, 256).sum(axis=0) * scale
    for i in range(2):
        for k in range(2):
            mine = (a == i) & (c == k) & (yl == c)
            copy = pltpu.make_async_remote_copy(
                src_ref=ssend.at[2 * i + k], dst_ref=rr.at[2 * a + yl],
                send_sem=sems.out(), recv_sem=fin_sem.at[2 * a + yl],
                device_id=dev(a=i, yl=c, c=k), device_id_type=MESH,
            )

            @pl.when(mine)
            def _():
                rr[2 * i + k] = ssend[2 * i + k]

            @pl.when(jnp.logical_not(mine))
            def _(copy=copy):
                copy.start()

            pending.append((mine, copy))
    for i in range(2):
        for k in range(2):
            mine = (a == i) & (c == yl) & (yl == k)

            @pl.when(jnp.logical_not(mine))
            def _():
                at = rr.at[2 * i + k]
                pltpu.make_async_copy(at, at, fin_sem.at[2 * i + k]).wait()

        o_ref[32 * i : 32 * i + 32] = rr[2 * i] + rr[2 * i + 1]
    for mine, copy in pending:

        @pl.when(jnp.logical_not(mine))
        def _(copy=copy):
            copy.wait_send()


def local(inputs, out_grads, basis_in, basis_out):
    scale = 1.0 / (inputs.shape[1] * lax.axis_size("ctx") * inputs.shape[0] * lax.axis_size("dp"))
    anywhere = pl.BlockSpec(memory_space=pl.ANY)
    return pl.pallas_call(
        functools.partial(kernel, scale),
        out_shape=jax.ShapeDtypeStruct((64, 256), F32),
        in_specs=[anywhere] * 4,
        out_specs=pl.BlockSpec(memory_space=pltpu.VMEM),
        scratch_shapes=[
            pltpu.VMEM((2, 4, 128, 1024), BF16),
            pltpu.VMEM((128, 1024), BF16),
            pltpu.VMEM((1024, 1024), BF16),
            pltpu.VMEM((8, 2, 256, 128), BF16),
            pltpu.VMEM((2, 2, 256, 128), BF16),
            pltpu.VMEM((8, 256, 128), BF16),
            pltpu.VMEM((8, 256, 128), BF16),
            pltpu.VMEM((8, 256, 128), F32),
            pltpu.VMEM((8, 256, 128), BF16),
            pltpu.VMEM((4, 8, 256, 128), BF16),
            pltpu.VMEM((4, 4, 1024, 256), BF16),
            pltpu.VMEM((4, 256, 256), F32),
            pltpu.VMEM((4, 32, 256), F32),
            pltpu.VMEM((4, 32, 256), F32),
            pltpu.SemaphoreType.DMA((N_SEND,)),
            pltpu.SemaphoreType.DMA((N_RECV,)),
            pltpu.SemaphoreType.DMA((4,)),
        ],
        compiler_params=pltpu.CompilerParams(
            collective_id=0, has_side_effects=True, vmem_limit_bytes=48 << 20
        ),
    )(inputs, out_grads, basis_in.reshape(4, 1024, 256), basis_out)


def solution(mesh):
    return jax.shard_map(
        local,
        mesh=mesh,
        in_specs=(P("dp", "ctx", None), P("dp", "ctx", None), P(None, "ctx"), P()),
        out_specs=P("dp", "ctx"),
        check_vma=False,
    )
```

time: 346 us -> 101 us (0.29)
  the two profiles are of different devices: /device:TPU:2 before, /device:TPU:1 now
where the time goes in v1:
time: 101 us
  Pallas kernels  95 us (94%)
  local copies, waits for them, and re-layouts  5.99 us (6%)
    pallas_call x1, Pallas kernels, local(): pl.pallas_call(functools.partial(kernel, scale), out_shape=jax.ShapeDtype...  95 us
    unnamed x9, local copies, waits for them, and re-layouts  5.99 us

profile of v1, /device:TPU:1, one launch (start us, length us, event | category | flops | bytes accessed | tf_op | source)
XLA Modules:
  0.0 101.0 jit_solution(7910921200002051619)
XLA Ops:
  0.0 0.0 copy-start
  0.0 1.6 %copy-done = bf16[4096,256]{1,0:T(8,128)(2,1)S(1)} copy-done((bf16[4096,256]{1,0:T(8,128)(2,1)S(1)}, bf16[4096,256]{1,0:T(8,128)(2,1)}, u32[]{:S(2)}) %copy-start) | copy-done | bytes 2097176
  1.6 0.0 copy-start.1
  1.6 1.6 %copy-done.1 = bf16[1024,1024]{1,0:T(8,128)(2,1)S(1)} copy-done((bf16[1024,1024]{1,0:T(8,128)(2,1)S(1)}, bf16[1024,1024]{1,0:T(8,128)(2,1)}, u32[]{:S(2)}) %copy-start.1) | copy-done | bytes 2097176
  3.2 0.0 copy-start.2
  3.2 1.2 %copy-done.2 = bf16[1,128,4096]{2,1,0:T(8,128)(2,1)S(1)} copy-done((bf16[1,128,4096]{2,1,0:T(8,128)(2,1)S(1)}, bf16[1,128,4096]{2,1,0:T(8,128)(2,1)}, u32[]{:S(2)}) %copy-start.2) | copy-done | bytes 1048600
  4.4 0.0 copy-start.3
  4.4 0.9 copy-done.3
  5.4 95.0 %shard_map.46 = f32[64,256]{1,0:T(8,128)S(1)} custom-call(bf16[1,128,4096]{2,1,0:T(8,128)(2,1)S(1)} %copy-done.2, bf16[1,128,1024]{2,1,0:T(8,128)(2,1)S(1)} %copy-done.3, bf16[4,1024,256]{2,1,0:T(8,128)(2,1)S(1)} %bitcast.1, bf16[1024,1024]{1,0:T(8,128)(2,1)S(1)} %copy-done.1), custom_call_target="tpu_custom_call" | custom-call | tf_op jit(solution)/shard_map/pallas_call | solution.py:310
  100.4 0.6 copy.6
Async XLA Ops:
  0.0 1.6 %copy-start = (bf16[4096,256]{1,0:T(8,128)(2,1)S(1)}, bf16[4096,256]{1,0:T(8,128)(2,1)}, u32[]{:S(2)}) copy-start(bf16[4096,256]{1,0:T(8,128)(2,1)} %param.6) | copy-start | bytes 6291460
  1.6 1.6 %copy-start.1 = (bf16[1024,1024]{1,0:T(8,128)(2,1)S(1)}, bf16[1024,1024]{1,0:T(8,128)(2,1)}, u32[]{:S(2)}) copy-start(bf16[1024,1024]{1,0:T(8,128)(2,1)} %bo_hbm.1) | copy-start | bytes 6291460
  3.2 1.2 %copy-start.2 = (bf16[1,128,4096]{2,1,0:T(8,128)(2,1)S(1)}, bf16[1,128,4096]{2,1,0:T(8,128)(2,1)}, u32[]{:S(2)}) copy-start(bf16[1,128,4096]{2,1,0:T(8,128)(2,1)} %x_hbm.1) | copy-start | bytes 3145732
  4.4 0.9 copy-start.3

commit v2 on v0

v2 whole, which is shorter than its diff:
```python
import functools
import math

import jax
import jax.numpy as jnp
from jax import lax
from jax.experimental import pallas as pl
from jax.experimental.pallas import tpu as pltpu
from jax.sharding import PartitionSpec as P

MESH = pl.DeviceIdType.MESH
BF16, F32 = jnp.bfloat16, jnp.float32
BLOCKS = 8
PIECES = 8
EARLY = 6
DIRECT = (6, 7)
N_SEND = 12
N_RECV = 80
VMEM = 63 << 20


def size(ref):
    return math.prod(ref.shape) * ref.dtype.itemsize


def kernel(
    scale, x_hbm, g_hbm, bi_hbm, bo_hbm, o_ref,
    xbuf, gbuf, bobuf, rbuf, rsend, psend, precv, pkeep, hz, hbuf, bbuf, acc, ssend, rr,
    send_sem, recv_sem, fin_sem,
):
    dp, ctx = lax.axis_index("dp"), lax.axis_index("ctx")
    yl, z = dp // 8, dp % 8
    a, b, c = ctx // 8, (ctx // 2) % 4, ctx % 2
    right, left, far = (b + 1) % 4, (b + 3) % 4, (b + 2) % 4
    own, partner = a * 2 + c, (1 - a) * 2 + c
    senders, receivers, sent, due = {}, {}, {}, {}

    def dev(a=a, yl=yl, z=z, b=b, c=c):
        return (yl * 8 + z, a * 8 + b * 2 + c)

    sibling = dev(c=1 - c)

    def out(kind):
        return send_sem.at[senders.setdefault(kind, len(senders))]

    def into(name):
        return recv_sem.at[receivers.setdefault(name, len(receivers))]

    def send(src, dst, to, *name):
        pltpu.make_async_remote_copy(
            src_ref=src, dst_ref=dst, send_sem=out(name[0]), recv_sem=into(name),
            device_id=to, device_id_type=MESH,
        ).start()
        sent[name[0]] = sent.get(name[0], 0) + size(src)
        due.setdefault(name, []).append(dst)

    def wait(ref, *name):
        assert size(ref) == sum(map(size, due.pop(name))), name
        pltpu.make_async_copy(ref, ref, into(name)).wait()

    def wait_sent(ref, kind):
        assert size(ref) == sent.pop(kind), kind
        pltpu.make_async_remote_copy(
            src_ref=ref, dst_ref=ref, send_sem=out(kind), recv_sem=recv_sem.at[0],
            device_id=sibling, device_id_type=MESH,
        ).wait_send()

    def local(src, dst, name):
        copy = pltpu.make_async_copy(src, dst, into(name))
        copy.start()
        return copy

    peers = [dev(b=(b + i) % 4, c=k) for i in (1, 3) for k in (0, 1)]
    peers += [dev(b=far), sibling]
    peers += [dev(z=(z + i) % 8) for i in range(1, 8)]
    peers += [
        dev(a=(a + i) % 2, yl=(yl + j) % 2, c=k)
        for i, j in ((0, 1), (1, 0), (1, 1))
        for k in (0, 1)
    ]
    barrier = pltpu.get_barrier_semaphore()
    for peer in peers:
        pl.semaphore_signal(barrier, inc=1, device_id=peer, device_id_type=MESH)
    features = pl.ds(pl.multiple_of(b * 1024, 1024), 1024)
    load_g = local(g_hbm.at[0], gbuf, "g")
    load_bo = local(bo_hbm, bobuf, "bo")
    load_x = local(x_hbm.at[0, :, features], xbuf.at[c, b], "x")
    load_bi = local(bi_hbm, bbuf.at[own], "bi")
    pl.semaphore_wait(barrier, len(peers))

    def at_lanes(j):
        return pl.ds(j * 128, 128)

    def at_rows(k):
        return pl.ds(pl.multiple_of(k * 32, 32), 32)

    def x_send(j):
        for to in (right, left, far):
            src = pl.ds(pl.multiple_of(to * 1024 + j * 128, 128), 128)
            send(x_hbm.at[0, :, src], xbuf.at[c, b, :, at_lanes(j)], dev(b=to), "X", j)

    def x_share(j):
        wait(xbuf.at[0, pl.ds(0, 3), :, at_lanes(j)], "X", j)
        at = (c, slice(None), slice(None), at_lanes(j))
        send(xbuf.at[at], xbuf.at[at], sibling, "XF", j)

    def b_at(k, g):
        rows = 1024 // PIECES
        return (2 * (z % 2) + k, pl.ds(g * rows, rows))

    def b_send(g):
        at = b_at(1 - yl, g)
        send(bi_hbm.at[at], bbuf.at[(own, *at)], dev(a=1 - a, yl=1 - yl), "B1", g)

    def b_forward(g):
        ref = bbuf.at[(partner, *b_at(yl, g))]
        wait(ref, "B1", g)
        send(ref, ref, dev(yl=1 - yl), "B2", g)
        send(ref, ref, dev(z=(z + 9 - 2 * yl) % 8), "BZ", int(g >= EARLY))

    def b_relay(g):
        ref = bbuf.at[(partner, *b_at(1 - yl, g))]
        wait(ref, "B2", g)
        send(ref, ref, dev(z=(z + 7 + 2 * yl) % 8), "BZ", int(g >= EARLY))

    def b_rows(h):
        rows = 1024 // PIECES
        return pl.ds(EARLY * rows, 1024 - EARLY * rows) if h else pl.ds(0, EARLY * rows)

    def b_share(h):
        wait(bbuf.at[partner, pl.ds(0, 2), b_rows(h)], "BZ", h)
        ref = bbuf.at[partner, :, b_rows(h)]
        send(ref, ref, sibling, "B3", h)

    def b_done(h):
        wait(bbuf.at[3 - own, :, b_rows(h)], "B3", h)

    def b_own_done():
        load_bi.wait()
        wait(bbuf.at[a * 2 + 1 - c], "B0")

    def b_own():
        send(bi_hbm, bbuf.at[own], sibling, "B0")

    slot = c * 4 + b

    def r_compute():
        load_g.wait()
        load_bo.wait()
        for k in range(2):
            rot = jnp.dot(
                gbuf[...], bobuf[:, 512 * k : 512 * k + 512], preferred_element_type=F32
            )
            turned = rot.T.astype(BF16).reshape(8, 2, 32, 128)
            for h in range(2):
                rsend[k, h] = turned[:, h].reshape(256, 128)

    def half(p):
        return a if p else 1 - a

    def r_send(p):
        h = half(p)
        for i, to in ((1, right), (3, left)):
            send(rsend.at[c, h], rbuf.at[slot, h], dev(b=to), "R", p, i)
            send(rsend.at[1 - c, h], rbuf.at[slot, h], dev(b=to, c=1 - c), "R", p, i)
        send(rsend.at[1 - c, h], rbuf.at[slot, h], sibling, "R", p, 2)
        rbuf[slot, h] = rsend[c, h]

    def r_forward(p):
        h = half(p)
        for i, origin, to, first in ((1, left, right, 0), (3, right, left, 4)):
            wait(rbuf.at[pl.ds(0, 2), 0], "R", p, i)
            block = rbuf.at[first + origin, h]
            send(block, block, dev(b=to), "R", p, 2)

    def r_done(p):
        wait(rbuf.at[pl.ds(0, 3), 0], "R", p, 2)

    def product(j, h):
        lhs = jnp.concatenate([rbuf[s, h] for s in range(8)], axis=1)
        rhs = xbuf[:, :, :, j * 128 : j * 128 + 128].reshape(1024, 128)
        return jnp.dot(lhs, rhs, preferred_element_type=F32)

    def theirs(j):
        wait(xbuf.at[1 - c, :, :, at_lanes(j)], "XF", j)
        psend[j] = product(j, 1 - a).astype(BF16)
        send(psend.at[j], precv.at[j], dev(a=1 - a), "P", j)

    def mine(j):
        pkeep[j] = product(j, a)

    def z_send(j):
        wait(precv.at[j], "P", j)
        hz[j] = (pkeep[j] + precv[j].astype(F32)).astype(BF16)
        for i in (4, 3, 5, 2, 6, 1, 7):
            to = (z + i) % 8
            send(hz.at[j, at_rows(to)], hbuf.at[b, j, at_rows(z)], dev(z=to), "Z", j)
        hbuf[b, j, at_rows(z)] = hz[j, at_rows(z)]

    def h_send(j):
        wait(hbuf.at[b, j, pl.ds(0, 224)], "Z", j)
        ref = hbuf.at[b, j]
        if j in DIRECT:
            send(ref, ref, dev(b=far), "HF", j)
        for to in (right, left):
            send(ref, ref, dev(b=to), "H", j)

    def h_wait(j):
        wait(hbuf.at[pl.ds(0, 2), j], "H", j)

    def h_forward(j):
        h_wait(j)
        for origin, to, first in ((left, right, 0), (right, left, 128)):
            part = hbuf.at[origin, j, pl.ds(first, 128)]
            send(part, part, dev(b=to), "HF", j)

    def tile_begin(j):
        if j in DIRECT:
            h_wait(j)
        wait(hbuf.at[far, j], "HF", j)
        return jnp.concatenate([hbuf[x, j] for x in range(4)], axis=1)

    def tile_term(j, k, lhs):
        rhs = bbuf[k, :, j * 128 : j * 128 + 128].reshape(512, 256)
        return jnp.dot(lhs, rhs, preferred_element_type=F32)

    def tile(j):
        lhs = tile_begin(j)
        for k in range(4):
            term = tile_term(j, k, lhs)
            acc[k] = term if j == 0 else acc[k] + term

    def wait_all_sent():
        wait_sent(xbuf.at[0, pl.ds(0, 3)], "X")
        wait_sent(xbuf.at[0], "XF")
        wait_sent(rbuf.at[pl.ds(0, 7)], "R")
        wait_sent(psend, "P")
        wait_sent(hz.at[pl.ds(0, 7)], "Z")
        wait_sent(hbuf.at[pl.ds(0, 2)], "H")
        wait_sent(hbuf.at[0], "HF")
        wait_sent(bbuf.at[0], "B0")
        wait_sent(bbuf.at[0, 0], "B1")
        wait_sent(bbuf.at[0, 0], "B2")
        wait_sent(bbuf.at[0, pl.ds(0, 2)], "BZ")
        wait_sent(bbuf.at[0], "B3")

    x_send(0)
    b_send(0)
    b_send(1)
    b_send(2)
    b_send(3)
    b_send(4)
    b_send(5)
    r_compute()
    r_send(0)
    r_send(1)
    b_own()
    load_x.wait()
    x_share(0)
    b_forward(0)
    r_forward(0)
    x_send(1)
    x_send(2)
    b_forward(1)
    b_forward(2)
    b_forward(3)
    b_relay(0)
    r_forward(1)
    x_send(3)
    x_send(4)
    x_send(5)
    x_send(6)
    x_send(7)
    b_forward(4)
    b_relay(1)
    r_done(0)
    theirs(0)
    b_forward(5)
    b_relay(2)
    x_share(1)
    theirs(1)
    b_relay(3)
    x_share(2)
    theirs(2)
    b_relay(4)
    r_done(1)
    mine(0)
    mine(1)
    b_relay(5)
    z_send(0)
    x_share(3)
    theirs(3)
    mine(2)
    z_send(1)
    x_share(4)
    theirs(4)
    mine(3)
    x_share(5)
    z_send(2)
    theirs(5)
    mine(4)
    h_send(0)
    x_share(6)
    h_send(1)
    theirs(6)
    mine(5)
    x_share(7)
    z_send(3)
    theirs(7)
    b_send(6)
    b_send(7)
    z_send(4)
    mine(6)
    h_send(2)
    mine(7)
    z_send(5)
    b_share(0)
    h_forward(0)
    z_send(6)
    h_send(3)
    h_forward(1)
    b_forward(6)
    z_send(7)
    h_send(4)
    b_forward(7)
    h_forward(2)
    b_own_done()
    b_done(0)
    tile(0)
    h_send(5)
    h_send(6)
    h_forward(3)
    b_relay(6)
    tile(1)
    h_send(7)
    b_relay(7)
    h_forward(4)
    tile(2)
    h_forward(5)
    b_share(1)
    tile(3)
    tile(4)
    tile(5)
    b_done(1)
    wait_all_sent()
    tile(6)

    copies = []
    last = tile_begin(BLOCKS - 1)
    for i in range(2):
        for k in range(2):
            part = acc[2 * i + k] + tile_term(BLOCKS - 1, 2 * i + k, last)
            ssend[2 * i + k] = (part * part).reshape(8, 32, 256).sum(axis=0) * scale
            stays = (a == i) & (c == k) & (yl == c)
            copy = pltpu.make_async_remote_copy(
                src_ref=ssend.at[2 * i + k], dst_ref=rr.at[2 * a + yl],
                send_sem=fin_sem.at[4 + 2 * i + k], recv_sem=fin_sem.at[2 * a + yl],
                device_id=dev(a=i, yl=c, c=k), device_id_type=MESH,
            )
            copies.append((stays, copy))

            @pl.when(stays)
            def _():
                rr[2 * i + k] = ssend[2 * i + k]

            @pl.when(jnp.logical_not(stays))
            def _():
                copy.start()

    for i in range(2):
        for k in range(2):

            @pl.when(jnp.logical_not((a == i) & (c == yl) & (yl == k)))
            def _():
                at = rr.at[2 * i + k]
                pltpu.make_async_copy(at, at, fin_sem.at[2 * i + k]).wait()

        o_ref[32 * i : 32 * i + 32] = rr[2 * i] + rr[2 * i + 1]
    for stays, copy in copies:

        @pl.when(jnp.logical_not(stays))
        def _():
            copy.wait_send()


def local(inputs, out_grads, basis_in, basis_out):
    scale = 1.0 / (inputs.shape[1] * lax.axis_size("ctx") * inputs.shape[0] * lax.axis_size("dp"))
    anywhere = pl.BlockSpec(memory_space=pl.ANY)
    return pl.pallas_call(
        functools.partial(kernel, scale),
        out_shape=jax.ShapeDtypeStruct((64, 256), F32),
        in_specs=[anywhere] * 4,
        out_specs=pl.BlockSpec(memory_space=pltpu.VMEM),
        scratch_shapes=[
            pltpu.VMEM((2, 4, 128, 1024), BF16),
            pltpu.VMEM((128, 1024), BF16),
            pltpu.VMEM((1024, 1024), BF16),
            pltpu.VMEM((8, 2, 256, 128), BF16),
            pltpu.VMEM((2, 2, 256, 128), BF16),
            pltpu.VMEM((8, 256, 128), BF16),
            pltpu.VMEM((8, 256, 128), BF16),
            pltpu.VMEM((8, 256, 128), F32),
            pltpu.VMEM((8, 256, 128), BF16),
            pltpu.VMEM((4, 8, 256, 128), BF16),
            pltpu.VMEM((4, 4, 1024, 256), BF16),
            pltpu.VMEM((4, 256, 256), F32),
            pltpu.VMEM((4, 32, 256), F32),
            pltpu.VMEM((4, 32, 256), F32),
            pltpu.SemaphoreType.DMA((N_SEND,)),
            pltpu.SemaphoreType.DMA((N_RECV,)),
            pltpu.SemaphoreType.DMA((8,)),
        ],
        compiler_params=pltpu.CompilerParams(
            collective_id=0, has_side_effects=True, vmem_limit_bytes=VMEM
        ),
    )(inputs, out_grads, basis_in.reshape(4, 1024, 256), basis_out)


def solution(mesh):
    return jax.shard_map(
        local,
        mesh=mesh,
        in_specs=(P("dp", "ctx", None), P("dp", "ctx", None), P(None, "ctx"), P()),
        out_specs=P("dp", "ctx"),
        check_vma=False,
    )
```

time: 346 us -> 64.2 us (0.19)
  the two profiles are of different devices: /device:TPU:2 before, /device:TPU:1 now
where the time goes in v2:
time: 64.2 us; the launch traced here: 64.1 us
  Pallas kernels  62.6 us (98%)
  local copies, waits for them, and re-layouts  1.47 us (2%)
    pallas_call x1, Pallas kernels, local(): pl.pallas_call(functools.partial(kernel, scale), out_shape=jax.ShapeDtype...  62.6 us
    unnamed x1, local copies, waits for them, and re-layouts  1.47 us

profile of v2, /device:TPU:1, one launch (start us, length us, event | category | flops | bytes accessed | tf_op | source)
XLA Modules:
  0.0 64.1 jit_solution(10327084288961053663)
XLA Ops:
  0.0 62.6 %shard_map.46 = f32[64,256]{1,0:T(8,128)} custom-call(bf16[1,128,4096]{2,1,0:T(8,128)(2,1)} %x_hbm.1, bf16[1,128,1024]{2,1,0:T(8,128)(2,1)} %g_hbm.1, bf16[4,1024,256]{2,1,0:T(8,128)(2,1)} %bitcast.1, bf16[1024,1024]{1,0:T(8,128)(2,1)} %bo_hbm.1), custom_call_target="tpu_custom_call" | custom-call | tf_op jit(solution)/shard_map/pallas_call | solution.py:389
  62.6 1.5 %copy.6 = f32[64,256]{1,0:T(8,128)} copy(f32[64,256]{1,0:T(8,128)} %shard_map.46) | data formatting | bytes 131072

commit v3 on v2

--- a/solution.py
+++ b/solution.py
@@ -13,10 +13,10 @@
 BLOCKS = 8
 PIECES = 8
 EARLY = 6
-DIRECT = (6, 7)
+DIRECT = (7,)
 N_SEND = 12
 N_RECV = 80
-VMEM = 63 << 20
+VMEM = 54976 << 10
 
 
 def size(ref):
@@ -339,6 +339,7 @@
     h_forward(5)
     b_share(1)
     tile(3)
+    h_forward(6)
     tile(4)
     tile(5)
     b_done(1)

time: 64.2 us -> 62.2 us (0.969)
  Pallas kernels: 62.6 us -> 61.5 us
  local copies, waits for them, and re-layouts: 1.47 us -> 0.63 us
    pallas_call x1, Pallas kernels: 62.6 us -> 61.5 us  [local(): pl.pallas_call(functools.partial(kernel, scale), out_shape=jax.ShapeDtype...]
    unnamed x1, local copies, waits for them, and re-layouts: 1.47 us -> 0.63 us
where the time goes in v3:
time: 62.2 us; the launch traced here: 62.1 us
  Pallas kernels  61.5 us (99%)
  local copies, waits for them, and re-layouts  0.63 us (1%)
    pallas_call x1, Pallas kernels, local(): pl.pallas_call(functools.partial(kernel, scale), out_shape=jax.ShapeDtype...  61.5 us

profile of v3, /device:TPU:1, one launch (start us, length us, event | category | flops | bytes accessed | tf_op | source)
XLA Modules:
  0.0 62.1 jit_solution(18091915115357711506)
XLA Ops:
  0.0 61.5 %shard_map.46 = f32[64,256]{1,0:T(8,128)S(1)} custom-call(bf16[1,128,4096]{2,1,0:T(8,128)(2,1)} %x_hbm.1, bf16[1,128,1024]{2,1,0:T(8,128)(2,1)} %g_hbm.1, bf16[4,1024,256]{2,1,0:T(8,128)(2,1)} %bitcast.1, bf16[1024,1024]{1,0:T(8,128)(2,1)} %bo_hbm.1), custom_call_target="tpu_custom_call" | custom-call | tf_op jit(solution)/shard_map/pallas_call | solution.py:390
  61.5 0.6 %copy.6 = f32[64,256]{1,0:T(8,128)} copy(f32[64,256]{1,0:T(8,128)S(1)} %shard_map.46) | data formatting | bytes 131072

commit v4 on v3

--- a/solution.py
+++ b/solution.py
@@ -83,9 +83,12 @@
         pl.semaphore_signal(barrier, inc=1, device_id=peer, device_id_type=MESH)
     features = pl.ds(pl.multiple_of(b * 1024, 1024), 1024)
     load_g = local(g_hbm.at[0], gbuf, "g")
-    load_bo = local(bo_hbm, bobuf, "bo")
-    load_x = local(x_hbm.at[0, :, features], xbuf.at[c, b], "x")
-    load_bi = local(bi_hbm, bbuf.at[own], "bi")
+    for i in range(4):
+        rows = pl.ds(256 * i, 256)
+        local(bo_hbm.at[rows], bobuf.at[rows], "bo")
+    load_bo = pltpu.make_async_copy(bo_hbm, bobuf, into("bo"))
+    load_x = pltpu.make_async_copy(x_hbm.at[0, :, features], xbuf.at[c, b], into("x"))
+    load_bi = pltpu.make_async_copy(bi_hbm, bbuf.at[own], into("bi"))
     pl.semaphore_wait(barrier, len(peers))
 
     def at_lanes(j):
@@ -147,6 +150,8 @@
     def r_compute():
         load_g.wait()
         load_bo.wait()
+        load_x.start()
+        load_bi.start()
         for k in range(2):
             rot = jnp.dot(
                 gbuf[...], bobuf[:, 512 * k : 512 * k + 512], preferred_element_type=F32
@@ -306,6 +311,7 @@
     mine(5)
     x_share(7)
     z_send(3)
+    b_share(0)
     theirs(7)
     b_send(6)
     b_send(7)
@@ -314,7 +320,6 @@
     h_send(2)
     mine(7)
     z_send(5)
-    b_share(0)
     h_forward(0)
     z_send(6)
     h_send(3)

time: 62.2 us -> 62.2 us (level)
  no operation moved by 1% of the time
where the time goes in v4:
time: 62.2 us; the launch traced here: 62.1 us
  Pallas kernels  61.5 us (99%)
  local copies, waits for them, and re-layouts  0.63 us (1%)
    pallas_call x1, Pallas kernels, local(): pl.pallas_call(functools.partial(kernel, scale), out_shape=jax.ShapeDtype...  61.5 us

profile of v4, /device:TPU:1, one launch (start us, length us, event | category | flops | bytes accessed | tf_op | source)
XLA Modules:
  0.0 62.1 jit_solution(12515810191765041773)
XLA Ops:
  0.0 61.5 %shard_map.46 = f32[64,256]{1,0:T(8,128)S(1)} custom-call(bf16[1,128,4096]{2,1,0:T(8,128)(2,1)} %x_hbm.1, bf16[1,128,1024]{2,1,0:T(8,128)(2,1)} %g_hbm.1, bf16[4,1024,256]{2,1,0:T(8,128)(2,1)} %bitcast.1, bf16[1024,1024]{1,0:T(8,128)(2,1)} %bo_hbm.1), custom_call_target="tpu_custom_call" | custom-call | tf_op jit(solution)/shard_map/pallas_call | solution.py:395
  61.5 0.6 %copy.6 = f32[64,256]{1,0:T(8,128)} copy(f32[64,256]{1,0:T(8,128)S(1)} %shard_map.46) | data formatting | bytes 131072
